TPU v7x, 128 devices: a whole 4x4x4 slice. The times are simulated.
128 devices in a mesh: seq: 16 (over z, x), eig: 8 (over y, core).
Axes of the slice: x: 4, y: 4, z: 4, core: 2. Of those that a mesh axis runs over, the one named last changes fastest.
Arguments:
- cand_act: bfloat16 [16, 1024, 2560], P('seq', 'eig'), may hold values from -6 to 6
- cand_grad: bfloat16 [16, 1024, 10240], P('seq', 'eig'), may hold values from -6 to 6
- query_act: bfloat16 [64, 32, 2560], P('seq'), may hold values from -6 to 6
- query_grad: bfloat16 [64, 32, 10240], P('seq', None, 'eig'), may hold values from -6 to 6
- act_basis: bfloat16 [2560, 2560], P('seq'), may hold values from -0.125 to 0.125
- grad_basis: bfloat16 [8, 1280, 1280], P('eig'), may hold values from -0.15625 to 0.15625
- eigvals: float32 [10240, 2560], P('eig'), may hold values from 0.25 to 4
- query_lists: int32 [16, 16], replicated, may hold values from 0 to 63, as said below
- valid_len: int32 [16], P('seq'), may hold values from 256 to 1024, as said below
Outputs:
- scores: float32 [16, 16], P('seq')
Inputs may be any that keep to these rules, and one draw needn't show every extreme that they name: `query_lists`: each row names 16 different queries: two of the 4 queries q with q // 4 = s, for each of 8 different s. `valid_len`: at least one sequence is valid in full.
All inputs are finite; a program needn't handle non-finite values.
Results may differ from a plain program's by a relative error of at most 0.0055.
Values may be sent and summed in bfloat16 or wider, within the bound.
A program may use at most 128 MiB of HBM per device.

v0:
```python
import math

import jax
import jax.numpy as jnp
from jax import lax
from jax.sharding import PartitionSpec as P

DW = 2560
FW = 10240
LEN = 1024
LQ = 32


def shards(
    cand_act,
    cand_grad,
    query_act,
    query_grad,
    act_basis,
    grad_basis,
    eigvals,
    query_lists,
    valid_len,
):
    position = lax.axis_index("seq")
    local_blocks = grad_basis.shape[0]
    block_width = grad_basis.shape[1]
    held_queries = query_act.shape[0]
    query_rows = query_act.shape[1]
    act_width = query_act.shape[2]
    factor = 1.0 / math.sqrt(FW * DW * LEN * LQ)

    def rotate_grad(grad_rows):
        shape_in = grad_rows.shape
        blocks = grad_rows.reshape((-1, local_blocks, block_width))
        rotated = jnp.einsum("rbi,bij->rbj", blocks, grad_basis, preferred_element_type=jnp.float32)
        return rotated.reshape(shape_in).astype(jnp.bfloat16)

    query_flat = query_act.reshape((-1, act_width))
    left_parts = (lax.all_gather(cand_act[0], "eig", axis=0, tiled=True), query_flat)
    shard_rows = lax.all_gather(act_basis, "seq", axis=0, tiled=True)
    rotated_parts = tuple(
        (
            jnp.dot(left_rows, shard_rows, preferred_element_type=jnp.float32)
            for left_rows in left_parts
        )
    )
    rot_act = rotated_parts[0].astype(jnp.bfloat16)
    rot_query_act = (
        rotated_parts[1].astype(jnp.bfloat16).reshape((held_queries, query_rows, act_width))
    )
    grouped = lax.all_to_all(cand_grad[0], "eig", split_axis=1, concat_axis=0, tiled=True)
    total_rows = grouped.shape[0]
    length = valid_len[0]
    keep_rows = (jnp.arange(total_rows, dtype=jnp.int32) < length).astype(jnp.bfloat16)
    masked_act = rot_act * keep_rows[:, None]
    rot_grad = rotate_grad(grouped)
    rot_query_grad = rotate_grad(query_grad)
    contract_rows = (((0,), (0,)), ((), ()))
    cross_block = lax.dot_general(
        rot_grad, masked_act, contract_rows, preferred_element_type=jnp.float32
    )
    scaled = (cross_block / eigvals).astype(jnp.bfloat16)
    picked = lax.dynamic_index_in_dim(query_lists, position, 0, keepdims=False)
    every_grad, every_act = (
        lax.all_gather(rot_query_grad, "seq", axis=0, tiled=True),
        lax.all_gather(rot_query_act, "seq", axis=0, tiled=True),
    )
    chosen_grad = jnp.take(every_grad, picked, axis=0)
    chosen_act = jnp.take(every_act, picked, axis=0)
    projected = jnp.einsum("ktj,ij->kti", chosen_act, scaled, preferred_element_type=jnp.float32)
    partial_value = jnp.sum(jnp.sum(projected * chosen_grad.astype(jnp.float32), axis=2), axis=1)
    totals = lax.psum(partial_value, "eig") * factor
    return totals[None, :]


def solution(mesh):
    placed = (
        P("seq", "eig", None),
        P("seq", "eig", None),
        P("seq", None, None),
        P("seq", None, "eig"),
        P("seq", None),
        P("eig", None, None),
        P("eig", None),
        P(),
        P("seq"),
    )
    return jax.shard_map(
        shards, mesh=mesh, in_specs=placed, out_specs=P("seq", None), check_vma=False
    )
```

profile of v0, /device:TPU:1, one launch (start us, length us, event | category | flops | bytes accessed | tf_op | source)
XLA Modules:
  0.0 317.6 jit_solution(17140057881780959551)
XLA Ops:
  6.5 0.0 copy-start
  6.5 0.0 all-gather.6.cloned.1.call-start
  6.5 0.7 all-gather.6.cloned.1.call-update
  7.3 0.0 all-gather.10.cloned.1.call-start
  7.3 1.2 copy-done
  8.5 2.3 fusion.13
  10.8 0.0 all-gather.10.cloned.1.call-update
  10.8 0.0 all-gather.12.cloned.1.call-start
  10.9 0.7 all-gather.12.cloned.1.call-update
  11.6 0.0 all-gather.8.cloned.1.call-start
  11.6 93.8 %all-gather.6.cloned.1.call-done = bf16[2560,2560]{1,0:T(8,128)(2,1)} async-done(((bf16[160,2560]{1,0:T(8,128)(2,1)}), bf16[2560,2560]{1,0:T(8,128)(2,1)}) %all-gather.6.cloned.1.call-update) | async-done | bytes 13107216 | tf_op jit(solution)/shard_map/all_gather | solution.py:41
  105.4 7.7 %convolution_convert_fusion.2 = bf16[128,2560]{1,0:T(8,128)(2,1)} fusion(bf16[128,2560]{1,0:T(8,128)(2,1)} %bitcast.53, bf16[2560,2560]{1,0:T(8,128)(2,1)} %all-gather.6.cloned.1.call-done), kind=kOutput, calls=%fused_computation.8 | convolution fusion | flops 1678049280 | bytes 14417920 | tf_op jit(solution)/shard_map/dot_general | solution.py:44
  113.1 0.0 all-gather.8.cloned.1.call-update
  113.1 4.4 %copy.12 = bf16[1,128,10240]{1,2,0:T(8,128)(2,1)} copy(bf16[1,128,10240]{2,1,0:T(8,128)(2,1)} %param.10) | data formatting | bytes 5242880 | tf_op args[1]
  117.6 5.0 %all-to-all-start = ((bf16[128,8,1280]{0,2,1:T(8,128)(2,1)}), bf16[128,8,1280]{0,2,1:T(8,128)(2,1)}, u32[]{:S(2)}, u32[]{:S(2)}) async-start(bf16[128,8,1280]{0,2,1:T(8,128)(2,1)} %bitcast.50), calls=%async_computation | async-start | bytes 5242880 | tf_op jit(solution)/shard_map/all_to_all | solution.py:52
  123.2 0.7 fusion.21
  123.9 0.7 compare_and_fusion
  124.6 30.0 %all-to-all-done = bf16[128,8,1280]{0,2,1:T(8,128)(2,1)} async-done(((bf16[128,8,1280]{0,2,1:T(8,128)(2,1)}), bf16[128,8,1280]{0,2,1:T(8,128)(2,1)}, u32[]{:S(2)}, u32[]{:S(2)}) %all-to-all-start) | async-done | bytes 2621472 | tf_op jit(solution)/shard_map/all_to_all | solution.py:52
  154.6 4.5 %copy.13 = bf16[8,128,1280]{2,1,0:T(8,128)(2,1)} copy(bf16[8,128,1280]{1,2,0:T(8,128)(2,1)} %bitcast.7) | data formatting | bytes 5242880 | tf_op jit(solution)/shard_map/all_to_all | solution.py:52
  159.1 6.7 %fusion.6 = bf16[1024,1280]{0,1:T(8,128)(2,1)} fusion(bf16[1024,1280]{1,0:T(8,128)(2,1)} %bitcast.51, bf16[1,1280,1280]{2,1,0:T(8,128)(2,1)S(1)} %copy-done), kind=kOutput, calls=%fused_computation.13 | convolution fusion | flops 3356753920 | bytes 8519680 | tf_op jit(solution)/shard_map/rbi,bij->rbj/dot_general | solution.py:36
  165.8 0.0 all-gather.10.cloned.1.call-done
  165.8 4.2 %gather_fusion.1 = bf16[16,32,1280]{2,1,0:T(8,128)(2,1)} fusion(bf16[64,32,1280]{2,1,0:T(8,128)(2,1)} %all-gather.10.cloned.1.call-done, s32[1024]{0:T(1024)S(1)} %pad_clamp_fusion), kind=kCustom, calls=%fused_computation.1 | custom fusion | bytes 2621504 | tf_op jit(solution)/shard_map/jit(_take)/gather | solution.py:69
  170.0 31.9 %all-gather.12.cloned.1.call-done = bf16[1,1024,2560]{2,1,0:T(8,128)(2,1)} async-done(((bf16[1,128,2560]{2,1,0:T(8,128)(2,1)}), bf16[1,1024,2560]{2,1,0:T(8,128)(2,1)}) %all-gather.12.cloned.1.call-update) | async-done | bytes 5242896 | tf_op jit(solution)/shard_map/all_gather | solution.py:40
  201.9 29.5 %fusion = bf16[1280,2560,1]{1,0,2:T(8,128)(2,1)} fusion(f32[1280,2560]{1,0:T(8,128)} %param.15, bf16[1024,1280]{0,1:T(8,128)(2,1)} %fusion.6, bf16[2560,2560]{1,0:T(8,128)(2,1)} %all-gather.6.cloned.1.call-done, bf16[1,1024,2560]{2,1,0:T(8,128)(2,1)} %all-gather.12.cloned.1.call-done, bf16[1024]{0:T(1024)(128)(2,1)S(1)} %fusion.20), kind=kOutput, calls=%fused_computation.3 | convolution fusion | flops 20144455680 | bytes 40634368 | tf_op jit(solution)/shard_map/dot_general | solution.py:60
  231.5 52.6 %all-gather.8.cloned.1.call-done = bf16[64,32,2560]{2,1,0:T(8,128)(2,1)} async-done(((bf16[4,32,2560]{2,1,0:T(8,128)(2,1)}), bf16[64,32,2560]{2,1,0:T(8,128)(2,1)}) %all-gather.8.cloned.1.call-update) | async-done | bytes 10485776 | tf_op jit(solution)/shard_map/all_gather | solution.py:67
  284.1 6.2 %gather_fusion = bf16[16,32,2560]{2,1,0:T(8,128)(2,1)} fusion(bf16[64,32,2560]{2,1,0:T(8,128)(2,1)} %all-gather.8.cloned.1.call-done, s32[1024]{0:T(1024)S(1)} %pad_clamp_fusion), kind=kCustom, calls=%fused_computation | custom fusion | bytes 5242944 | tf_op jit(solution)/shard_map/jit(_take)/gather | solution.py:70
  290.3 0.0 copy-start.1
  290.3 7.8 %fusion.16 = f32[16]{0:T(128)S(1)} fusion(bf16[1280,2560,1]{1,0,2:T(8,128)(2,1)} %fusion, bf16[16,32,2560]{2,1,0:T(8,128)(2,1)} %gather_fusion, pred[16]{0:T(512)(128)(4,1)S(1)} %compare_and_fusion, bf16[16,32,1280]{2,1,0:T(8,128)(2,1)} %gather_fusion.1), kind=kOutput, calls=%fused_computation.17 | convolution fusion | flops 3359375360 | bytes 10485840 | tf_op jit(solution)/shard_map/ktj,ij->kti/dot_general | solution.py:71
  298.1 12.4 %psum.7 = f32[16]{0:T(128)S(1)} all-reduce(f32[16]{0:T(128)S(1)} %fusion.16), channel_id=1, replica_groups=mesh['seq'=16,'eig'=8] {'eig'}, use_global_device_ids=true, to_apply=%region_1.2 | all-reduce | flops 16 | bytes 128 | tf_op jit(solution)/shard_map/psum | solution.py:73
  310.5 0.5 multiply_bitcast_fusion
  311.0 0.0 copy-done.1
  (2 shorter events, 0.0 us)
Async XLA Ops:
  6.5 1.9 copy-start
  6.5 98.9 %all-gather.6.cloned.1.call-start = ((), (), s32[]{:S(2)}) async-start(), calls=%async_computation.1 | async-start | bytes 13926400 | tf_op jit(solution)/shard_map/all_gather | solution.py:41
  7.3 158.6 %all-gather.10.cloned.1.call-start = ((), (), s32[]{:S(2)}) async-start(), calls=%async_computation.3 | async-start | bytes 5570560 | tf_op jit(solution)/shard_map/all_gather | solution.py:66
  10.8 191.1 %all-gather.12.cloned.1.call-start = ((), (), s32[]{:S(2)}) async-start(), calls=%async_computation.4 | async-start | bytes 5898240 | tf_op jit(solution)/shard_map/all_gather | solution.py:40
  11.6 272.5 %all-gather.8.cloned.1.call-start = ((), (), s32[]{:S(2)}) async-start(), calls=%async_computation.2 | async-start | bytes 11141120 | tf_op jit(solution)/shard_map/all_gather | solution.py:67
  117.6 37.0 %all-to-all-start = ((bf16[128,8,1280]{0,2,1:T(8,128)(2,1)}), bf16[128,8,1280]{0,2,1:T(8,128)(2,1)}, u32[]{:S(2)}, u32[]{:S(2)}) async-start(bf16[128,8,1280]{0,2,1:T(8,128)(2,1)} %bitcast.50), calls=%async_computation | async-start | bytes 5242880 | tf_op jit(solution)/shard_map/all_to_all | solution.py:52
  290.3 20.7 %copy-start.1 = (bf16[1,1280,1280]{2,1,0:T(8,128)(2,1)S(1)}, bf16[1,1280,1280]{2,1,0:T(8,128)(2,1)}, u32[]{:S(2)}) copy-start(bf16[1,1280,1280]{2,1,0:T(8,128)(2,1)} %param.14) | copy-start | bytes 9830404
Sparse Core Ops, SparseCore 0:
  9.5 95.9 all-gather.5
  107.6 56.0 all-gather.9
  165.4 36.5 all-gather.11
  203.9 80.1 all-gather.7
where the time goes:
time: 320 us; the launch traced here: 318 us
  waiting for transfers between devices  210 us (66%)
  matrix products  54.1 us (17%)
  local copies, waits for them, and re-layouts  20.5 us (6%)
  between operations  13.8 us (4%)
  blocking collectives  12.4 us (4%)
  starting transfers between devices  5.09 us (2%)
    all_gather x1, waiting for transfers between devices, shards(): shard_rows = lax.all_gather(act_basis, 'seq', axis=0, tiled=True)  93.8 us
    all_gather x1, waiting for transfers between devices, shards(): lax.all_gather(rot_query_act, 'seq', axis=0, tiled=True)  52.6 us
    all_gather x1, waiting for transfers between devices, shards(): lax.all_gather(cand_act[0], 'eig', axis=0, tiled=True)  31.9 us
    all_to_all x1, waiting for transfers between devices, shards(): lax.all_to_all(cand_grad[0], 'eig', split_axis=1, concat_axis=0, tiled=True)  30 us
    dot_general x1, matrix products, shards(): lax.dot_general(rot_grad, masked_act, contract_rows, preferred_element_ty...  29.5 us
    psum x1, blocking collectives, shards(): totals = lax.psum(partial_value, 'eig') * factor  12.4 us
    dot_general x2, matrix products, rotate_grad(): jnp.einsum('rbi,bij->rbj', blocks, grad_basis, preferred_element_type=jnp...  9.07 us
    dot_general x1, matrix products, shards(): jnp.einsum('ktj,ij->kti', chosen_act, scaled, preferred_element_type=jnp....  7.78 us
  transfers between devices with their start and end apart: 5, of which 4 were waited for; matrix products, arithmetic and copies ran while one was open for 19% of the time, Pallas kernels for 0%

commit v1 on v0

v1 whole, which is shorter than its diff:
```python
import functools
import math

import jax
import jax.numpy as jnp
from jax import lax
from jax.experimental import pallas as pl
from jax.experimental.pallas import tpu as pltpu
from jax.sharding import PartitionSpec as P

DW = 2560
FW = 10240
LEN = 1024
LQ = 32
KQ = 16
GB = 1280
HALF = 1280
BF = jnp.bfloat16
F32 = jnp.float32
MESH = pl.DeviceIdType.MESH
FACTOR = 1.0 / math.sqrt(FW * DW * LEN * LQ)
CUTS = ((0, 768), (768, 512))
LANES = (0, -1, 1, 2)


def wrap(i):
    return lax.rem(i + 8, 4)


def mm(a, b, dims=((1,), (0,))):
    return lax.dot_general(a, b, (dims, ((), ())), preferred_element_type=F32)


def kernel(
    lists, lens, cand_act, cand_grad, query_act, query_grad, act_basis, grad_basis, eigvals,
    out,
    basis, rows, act, grads, rot_t, gbasis, recip, scaled, all_grad, slim, chosen, proj,
    raw_act, raw_grad, part,
    loc, bs, br, gs, gr, cs, cr, as_, ar, qs, qr, hs, hr, ts, tr, ps, pr,
):
    s = lax.axis_index("seq")
    e = lax.axis_index("eig")
    z, x = lax.div(s, 4), lax.rem(s, 4)
    y, h = lax.div(e, 2), lax.rem(e, 2)

    def slot(da, db):
        return 4 * wrap(z + h * da + (1 - h) * db) + wrap(x + (1 - h) * da + h * db)

    def on_seq(da, db):
        return {"seq": slot(da, db), "eig": e}

    def on_y(d):
        return {"seq": s, "eig": 2 * wrap(y + d) + h}

    def on_eig(d):
        return {"seq": s, "eig": lax.rem(e + d, 8)}

    sibling = {"seq": s, "eig": 2 * y + 1 - h}

    def remote(src, dst, send, recv, device):
        copy = pltpu.make_async_remote_copy(
            src_ref=src, dst_ref=dst, send_sem=send, recv_sem=recv,
            device_id=device, device_id_type=MESH,
        )
        copy.start()
        sent.append(copy)
        return copy

    sent = []

    my_cols = pl.ds(pl.multiple_of(h * HALF, 128), HALF)
    my_rows = pl.ds(pl.multiple_of(h * 128, 128), 128)
    local = [
        pltpu.make_async_copy(act_basis.at[:, my_cols], basis.at[s], loc.at[0]),
        pltpu.make_async_copy(query_act, raw_act, loc.at[1]),
        pltpu.make_async_copy(query_grad, raw_grad, loc.at[2]),
        pltpu.make_async_copy(grad_basis.at[0], gbasis, loc.at[3]),
        pltpu.make_async_copy(cand_act.at[0], rows.at[my_rows], loc.at[4]),
        pltpu.make_async_copy(
            cand_grad.at[0, :, pl.ds(pl.multiple_of(e * GB, 128), GB)], grads.at[e], loc.at[5]
        ),
        pltpu.make_async_copy(eigvals, recip, loc.at[6]),
    ]
    for copy in local:
        copy.start()

    barrier = pltpu.get_barrier_semaphore()
    greeted = [on_seq(1, 0), on_seq(-1, 0), on_seq(0, 1), on_seq(0, -1)]
    greeted += [on_eig(d) for d in range(1, 8)]
    for device in greeted:
        pl.semaphore_signal(barrier, inc=1, device_id=device, device_id_type=MESH)
    pl.semaphore_wait(barrier, len(greeted))

    def torus(view, own, send, recv):
        def ship(n, src, where, part, device):
            return remote(src, view(where, part), send.at[n], recv.at[n], device)

        ring = {}
        ring[0] = ship(0, own, s, None, on_seq(1, 0))
        ring[1] = ship(1, own, s, None, on_seq(-1, 0))
        for side, db in ((0, 1), (1, -1)):
            ring[4 + side] = ship(4 + side, own, s, None, on_seq(0, db))
        yield

        def second(lane):
            da = LANES[lane]
            where = slot(da, 0)
            for side, db in ((0, 1), (1, -1)):
                n = 4 + 4 * lane + side
                ring[n] = ship(n, view(where, None), where, None, on_seq(0, db))

        def onward(lane):
            da = LANES[lane]
            for side, db in ((0, 1), (1, -1)):
                ring[4 + 4 * lane + side].wait_recv()
                where = slot(da, -db)
                n = 6 + 4 * lane + side
                ring[n] = ship(n, view(where, side), where, side, on_seq(0, db))

        for side, da in ((0, 1), (1, -1)):
            ring[side].wait_recv()
            where = slot(-da, 0)
            ring[2 + side] = ship(2 + side, view(where, side), where, side, on_seq(da, 0))
            second(1 + side)
            yield
        onward(0)
        yield
        ring[2].wait_recv()
        ring[3].wait_recv()
        second(3)
        yield
        onward(1)
        yield
        onward(2)
        yield
        onward(3)
        yield
        for lane in range(4):
            ring[6 + 4 * lane].wait_recv()
            ring[7 + 4 * lane].wait_recv()
        yield

    def along_y(view, send, recv):
        def ship(n, half, where, part, device):
            ref = view(half, where, part)
            return remote(ref, ref, send.at[n], recv.at[n], device)

        got = [
            ship(0, h, y, None, on_y(1)),
            ship(1, h, y, None, on_y(-1)),
        ]
        across = [ship(4, h, y, None, sibling)]
        yield
        for side, d in ((0, 1), (1, -1)):
            got[side].wait_recv()
            where = wrap(y - d)
            got.append(ship(2 + side, h, where, side, on_y(d)))
            across.append(ship(5 + side, h, where, None, sibling))
        yield
        got[2].wait_recv()
        got[3].wait_recv()
        across.append(ship(7, h, wrap(y + 2), None, sibling))
        yield
        for copy in across:
            copy.wait_recv()
        yield

    def basis_view(where, part):
        return basis.at[where] if part is None else basis.at[where, pl.ds(80 * part, 80)]

    basis_run = torus(basis_view, act_basis.at[:, my_cols], bs, br)
    next(basis_run)

    rows_in = remote(cand_act.at[0], rows.at[my_rows], cs.at[0], cr.at[0], sibling)
    grads_in = []
    for d in (1, 7, 2, 6, 3, 5, 4):
        to = lax.rem(e + d, 8)
        cols = pl.ds(pl.multiple_of(to * GB, 128), GB)
        grads_in.append(
            remote(cand_grad.at[0, :, cols], grads.at[e], gs.at[d], gr.at[d], on_eig(d))
        )

    local[1].wait()
    r = lax.broadcasted_iota(jnp.int32, (32, 128), 0)
    c = lax.broadcasted_iota(jnp.int32, (32, 128), 1)
    want = lax.div(r, 8) * 32 + 8 * y + lax.rem(r, 8)
    pick = jnp.where(c == want, 1.0, 0.0).astype(BF)
    rows[256:288, :] = mm(pick, raw_act[...].reshape(128, DW)).astype(BF)

    local[2].wait()
    local[3].wait()
    own_grad = pl.ds(4 * s, 4)
    all_grad[own_grad] = (
        mm(raw_grad[...].reshape(128, GB), gbasis[...]).astype(BF).reshape(4, LQ, GB)
    )
    local[0].wait()
    local[6].wait()

    def invert(first, count):
        def body(i, carry):
            at = pl.ds(pl.multiple_of(i * 64, 64), 64)
            recip[at, :] = 1.0 / recip[at, :]
            return carry

        lax.fori_loop(first, first + count, body, 0)

    invert(0, 7)
    next(basis_run)
    next(basis_run)
    next(basis_run)
    invert(7, 7)
    next(basis_run)
    invert(14, 6)
    next(basis_run)
    next(basis_run)
    next(basis_run)

    local[5].wait()
    for copy in grads_in:
        copy.wait_recv()

    def rotate_grads(i, carry):
        block = grads[pl.ds(2 * i, 2)].reshape(256, GB)
        turned = mm(block, gbasis[...]).astype(BF)
        rot_t[:, pl.ds(pl.multiple_of(i * 256, 256), 256)] = turned.T
        return carry

    lax.fori_loop(0, 4, rotate_grads, 0)

    next(basis_run)

    local[4].wait()
    rows_in.wait_recv()
    length = lens[0]
    token = 256 * y + lax.broadcasted_iota(jnp.int32, (256, 1), 0)
    mine = pl.ds(pl.multiple_of(256 * y, 256), 256)
    act_runs = []

    def act_view(first, width, half, where, part):
        if part is None:
            at = pl.ds(pl.multiple_of(256 * where, 256), 256)
        else:
            at = pl.ds(pl.multiple_of(256 * where + 128 * part, 128), 128)
        return act.at[half, at, pl.ds(first, width)]

    for n, (first, width) in enumerate(CUTS):
        cols = pl.ds(first, width)
        turned = mm(rows[...], basis[:, :, cols].reshape(DW, width)).astype(BF)
        act[h, mine, cols] = jnp.where(token < length, turned[:256], jnp.zeros((), BF))
        slim[s, :, cols] = turned[256:]
        run = along_y(functools.partial(act_view, first, width), as_.at[n], ar.at[n])
        next(run)
        act_runs.append(run)

    def slim_view(where, part):
        return slim.at[where] if part is None else slim.at[where, pl.ds(16 * part, 16)]

    def grad_view(where, part):
        if part is None:
            return all_grad.at[pl.ds(4 * where, 4)]
        return all_grad.at[pl.ds(4 * where + 2 * part, 2)]

    slim_run = torus(slim_view, slim.at[s], qs, qr)
    next(slim_run)
    grad_run = torus(grad_view, grad_view(s, None), hs, hr)
    next(grad_run)
    for _ in range(8):
        next(slim_run)

    c = lax.broadcasted_iota(jnp.int32, (8, 512), 1)
    r = lax.broadcasted_iota(jnp.int32, (8, 512), 0)
    pick = jnp.concatenate(
        [jnp.where(c == lists[s, k] * 8 + r, 1.0, 0.0) for k in range(KQ)], axis=0
    ).astype(BF)
    chosen[h, y] = mm(pick, slim[...].reshape(512, HALF)).astype(BF)

    def chosen_view(half, where, part):
        if part is None:
            return chosen.at[half, where]
        return chosen.at[half, where, pl.ds(64 * part, 64)]

    chosen_run = along_y(chosen_view, ts, tr)
    next(chosen_run)

    def cross(half, first, count):
        def body(i, carry):
            cols = pl.ds(pl.multiple_of(i * 256, 256), 256)
            wide = pl.ds(pl.multiple_of(half * HALF + i * 256, 256), 256)
            block = mm(rot_t[...], act[half, :, cols])
            scaled[:, wide] = (block * recip[:, wide]).astype(BF)
            return carry

        lax.fori_loop(first, first + count, body, 0)

    next(grad_run)
    next(grad_run)
    next(act_runs[0])
    next(grad_run)
    next(grad_run)
    next(act_runs[0])
    next(act_runs[1])
    next(grad_run)
    next(act_runs[0])
    cross(0, 0, 3)
    next(chosen_run)
    next(grad_run)
    next(act_runs[1])
    next(grad_run)
    cross(1, 0, 3)
    next(chosen_run)
    next(act_runs[1])
    cross(0, 3, 2)
    cross(1, 3, 2)
    next(chosen_run)

    def project(i, carry):
        at = pl.ds(pl.multiple_of(i * 256, 256), 256)
        total = mm(chosen[0].reshape(512, HALF), scaled[at, :HALF], ((1,), (1,)))
        total += mm(chosen[1].reshape(512, HALF), scaled[at, HALF:], ((1,), (1,)))
        proj[:, :, at] = total.reshape(4, 128, 256)
        return carry

    lax.fori_loop(0, 5, project, 0)
    next(grad_run)

    def score(k, carry):
        grad = all_grad[lists[s, k]].astype(F32)
        at = pl.ds(pl.multiple_of(8 * k, 8), 8)
        total = proj[0, at] * grad[0:8]
        for n in range(1, 4):
            total += proj[n, at] * grad[8 * n : 8 * n + 8]
        folded = total[:, :128]
        for n in range(1, GB // 128):
            folded += total[:, 128 * n : 128 * n + 128]
        part[e, pl.ds(k, 1), :] = jnp.sum(folded, axis=0, keepdims=True)
        return carry

    lax.fori_loop(0, KQ, score, 0)

    parts_in = [
        remote(part.at[e], part.at[e], ps.at[d], pr.at[d], on_eig(d))
        for d in range(1, 8)
    ]
    for copy in parts_in:
        copy.wait_recv()
    full = part[0]
    for block in range(1, 8):
        full += part[block]
    full = jnp.concatenate([full, jnp.zeros((128 - KQ, 128), F32)], axis=0)
    out[...] = (jnp.sum(full.T, axis=0, keepdims=True) * FACTOR)[:, :KQ]

    for copy in sent:
        copy.wait_send()


def shards(
    cand_act, cand_grad, query_act, query_grad, act_basis, grad_basis, eigvals, query_lists,
    valid_len,
):
    anywhere = pl.BlockSpec(memory_space=pl.ANY)
    scalars = pl.BlockSpec(memory_space=pltpu.SMEM)
    dma = pltpu.SemaphoreType.DMA
    return pl.pallas_call(
        kernel,
        out_shape=jax.ShapeDtypeStruct((1, KQ), F32),
        in_specs=[scalars, scalars] + [anywhere] * 7,
        out_specs=pl.BlockSpec(memory_space=pltpu.VMEM),
        scratch_shapes=[
            pltpu.VMEM((16, 160, HALF), BF),
            pltpu.VMEM((288, DW), BF),
            pltpu.VMEM((2, LEN, HALF), BF),
            pltpu.VMEM((8, 128, GB), BF),
            pltpu.VMEM((GB, LEN), BF),
            pltpu.VMEM((GB, GB), BF),
            pltpu.VMEM((GB, DW), F32),
            pltpu.VMEM((GB, DW), BF),
            pltpu.VMEM((64, LQ, GB), BF),
            pltpu.VMEM((16, 32, HALF), BF),
            pltpu.VMEM((2, 4, 128, HALF), BF),
            pltpu.VMEM((4, 128, GB), F32),
            pltpu.VMEM((4, LQ, DW), BF),
            pltpu.VMEM((4, LQ, GB), BF),
            pltpu.VMEM((8, KQ, 128), F32),
            dma((7,)),
            dma((20,)), dma((20,)),
            dma((8,)), dma((8,)),
            dma((1,)), dma((1,)),
            dma((2, 8)), dma((2, 8)),
            dma((20,)), dma((20,)),
            dma((20,)), dma((20,)),
            dma((8,)), dma((8,)),
            dma((8,)), dma((8,)),
        ],
        compiler_params=pltpu.CompilerParams(
            collective_id=0, has_side_effects=True, vmem_limit_bytes=63 * 2**20
        ),
        name="influence",
    )(
        query_lists, valid_len, cand_act, cand_grad, query_act, query_grad, act_basis,
        grad_basis, eigvals,
    )


def solution(mesh):
    placed = (
        P("seq", "eig", None),
        P("seq", "eig", None),
        P("seq", None, None),
        P("seq", None, "eig"),
        P("seq", None),
        P("eig", None, None),
        P("eig", None),
        P(),
        P("seq"),
    )
    return jax.shard_map(
        shards, mesh=mesh, in_specs=placed, out_specs=P("seq", None), check_vma=False
    )
```

time: 320 us -> 105 us (0.33)
  waiting for transfers between devices: 210 us -> 0 us
  Pallas kernels: 0 us -> 103 us
  matrix products: 54.1 us -> 0 us
  local copies, waits for them, and re-layouts: 20.5 us -> 1.19 us
  between operations: 13.8 us -> 0.66 us
  blocking collectives: 12.4 us -> 0 us
  starting transfers between devices: 5.09 us -> 0 us
    all_gather x4 -> x0, waiting for transfers between devices: 178 us -> none  [the longest x1 93.8 us: shards(): shard_rows = lax.all_gather(act_basis, 'seq', axis=0, tiled=True)]
    pallas_call x0 -> x1, Pallas kernels: none -> 103 us  [shards(): pl.pallas_call(kernel, out_shape=jax.ShapeDtypeStruct((1, KQ), F32), in_s...]
    dot_general x5 -> x0, matrix products: 54.1 us -> none  [the longest x1 29.5 us: shards(): lax.dot_general(rot_grad, masked_act, contract_rows, preferred_element_ty...]
    all_to_all x1 -> x0, waiting for transfers between devices: 30 us -> none  [shards(): lax.all_to_all(cand_grad[0], 'eig', split_axis=1, concat_axis=0, tiled=True)]
    psum x1 -> x0, blocking collectives: 12.4 us -> none  [shards(): totals = lax.psum(partial_value, 'eig') * factor]
    gather x2 -> x0, local copies, waits for them, and re-layouts: 10.4 us -> none  [the longest x1 6.21 us: shards(): chosen_act = jnp.take(every_act, picked, axis=0)]
    all_to_all x1 -> x0, starting transfers between devices: 4.97 us -> none  [shards(): lax.all_to_all(cand_grad[0], 'eig', split_axis=1, concat_axis=0, tiled=True)]
    all_to_all x1 -> x0, local copies, waits for them, and re-layouts: 4.47 us -> none  [shards(): lax.all_to_all(cand_grad[0], 'eig', split_axis=1, concat_axis=0, tiled=True)]
  transfers between devices with their start and end apart: 5 -> 0, of which waited for: 4 -> 0; matrix products, arithmetic and copies ran while one was open for 19% -> 0% of each run, Pallas kernels for 0% -> 0%
where the time goes in v1:
time: 105 us
  Pallas kernels  103 us (98%)
  local copies, waits for them, and re-layouts  1.19 us (1%)
    pallas_call x1, Pallas kernels, shards(): pl.pallas_call(kernel, out_shape=jax.ShapeDtypeStruct((1, KQ), F32), in_s...  103 us

profile of v1, /device:TPU:1, one launch (start us, length us, event | category | flops | bytes accessed | tf_op | source)
XLA Modules:
  0.0 104.8 jit_solution(7550513398321010175)
XLA Ops:
  0.7 102.9 %influence.1 = f32[1,16]{1,0:T(1,128)} custom-call(s32[16,16]{1,0:T(8,128)} %lists.1, s32[1]{0:T(128)S(6)} %copy.11.lens, bf16[1,128,2560]{2,1,0:T(8,128)(2,1)} %cand_act.1, bf16[1,128,10240]{2,1,0:T(8,128)(2,1)} %cand_grad.1, bf16[4,32,2560]{2,1,0:T(8,128)(2,1)} %query_act.1, bf16[4,32,1280]{2,1,0:T(8,128)(2,1)} %query_grad.1, bf16[160,2560]{1,0:T(8,128)(2,1)} %act_basis.1, ...), custom_call_target="tpu_custom_call" | custom-call | tf_op jit(solution)/shard_map/influence/pallas_call | solution.py:363
  103.6 1.2 %copy.12 = f32[1,16]{1,0:T(1,128)} copy(f32[1,16]{1,0:T(1,128)} %influence.1) | data formatting | bytes 128

commit v2 on v1

v2 whole, which is shorter than its diff:
```python
import functools
import math

import jax
import jax.numpy as jnp
from jax import lax
from jax.experimental import pallas as pl
from jax.experimental.pallas import tpu as pltpu
from jax.sharding import PartitionSpec as P

DW = 2560
FW = 10240
LEN = 1024
LQ = 32
KQ = 16
GB = 1280
HALF = 1280
QUARTER = 640
BF = jnp.bfloat16
F32 = jnp.float32
MESH = pl.DeviceIdType.MESH
FACTOR = 1.0 / math.sqrt(FW * DW * LEN * LQ)
ORDER = (
    "brGwbbbbirGbbbib",
    "gMasigissssssagsgskgtg",
    "tatgaXgaxxkaqaXpg",
)
LANES = (0, -1, 1, 2)


def wrap(i):
    return lax.rem(i + 8, 4)


def mm(a, b, dims=((1,), (0,))):
    return lax.dot_general(a, b, (dims, ((), ())), preferred_element_type=F32)


def kernel(
    lists, lens, cand_act, cand_grad, query_act, query_grad, act_basis, grad_basis, eigvals,
    out,
    basis, rows, total, act, grads, rot_t, gbasis, recip, scaled, all_grad, slim, chosen, proj, begun,
    raw_grad, part,
    loc, bs, br, gs, gr, cs, cr, as_, ar, qs, qr, hs, hr, ts, tr, ps, pr,
):
    s = lax.axis_index("seq")
    e = lax.axis_index("eig")
    z, x = lax.div(s, 4), lax.rem(s, 4)
    y, h = lax.div(e, 2), lax.rem(e, 2)
    parity = lax.rem(y, 2)
    other = 1 - parity
    lower = 1 - lax.rem(y + h, 2)

    def slot(da, db):
        return 4 * wrap(z + h * da + (1 - h) * db) + wrap(x + (1 - h) * da + h * db)

    def on_seq(da, db):
        return {"seq": slot(da, db), "eig": e}

    def on_y(d):
        return {"seq": s, "eig": 2 * wrap(y + d) + h}

    def on_eig(d):
        return {"seq": s, "eig": lax.rem(e + d, 8)}

    sibling = {"seq": s, "eig": 2 * y + 1 - h}

    def remote(src, dst, send, recv, device):
        copy = pltpu.make_async_remote_copy(
            src_ref=src, dst_ref=dst, send_sem=send, recv_sem=recv,
            device_id=device, device_id_type=MESH,
        )
        copy.start()
        sent.append(copy)
        return copy

    sent = []

    def at_rows(i):
        return pl.ds(pl.multiple_of(128 * i, 128), 128)

    quarter = pl.ds(pl.multiple_of(parity * HALF + h * QUARTER, 128), QUARTER)
    block_rows = pl.ds(pl.multiple_of(160 * s, 32), 160)
    place = 2 * wrap(y - 1 + lower) + 1 - lower
    local = [
        pltpu.make_async_copy(act_basis.at[:, quarter], basis.at[block_rows], loc.at[0]),
        pltpu.make_async_copy(query_grad, raw_grad, loc.at[1]),
        pltpu.make_async_copy(grad_basis.at[0], gbasis, loc.at[2]),
        pltpu.make_async_copy(cand_act.at[0], rows.at[at_rows(1 + lower)], loc.at[3]),
        pltpu.make_async_copy(
            cand_grad.at[0, :, pl.ds(pl.multiple_of(e * GB, 128), GB)], grads.at[place], loc.at[4]
        ),
        pltpu.make_async_copy(eigvals, recip, loc.at[5]),
    ]
    local += [
        pltpu.make_async_copy(query_act.at[n], rows.at[pl.ds(512 + LQ * n, LQ)], loc.at[6 + n])
        for n in range(4)
    ]

    barrier = pltpu.get_barrier_semaphore()
    greeted = [on_seq(1, 0), on_seq(-1, 0), on_seq(0, 1), on_seq(0, -1)]
    greeted += [on_eig(d) for d in range(1, 8)]
    for device in greeted:
        pl.semaphore_signal(barrier, inc=1, device_id=device, device_id_type=MESH)
    pl.semaphore_wait(barrier, len(greeted))

    def torus(view_of, own_of, send, recv, width=QUARTER):
        cols = pl.ds(0, width)
        view = functools.partial(view_of, cols)
        own = own_of(cols)

        def ship(n, src, where, part, device):
            return remote(src, view(where, part), send.at[n], recv.at[n], device)

        ring = {}
        ring[0] = ship(0, own, s, None, on_seq(1, 0))
        ring[1] = ship(1, own, s, None, on_seq(-1, 0))
        for side, db in ((0, 1), (1, -1)):
            ring[4 + side] = ship(4 + side, own, s, None, on_seq(0, db))
        yield

        def second(lane):
            da = LANES[lane]
            where = slot(da, 0)
            for side, db in ((0, 1), (1, -1)):
                n = 4 + 4 * lane + side
                ring[n] = ship(n, view(where, None), where, None, on_seq(0, db))

        def onward(lane):
            da = LANES[lane]
            for side, db in ((0, 1), (1, -1)):
                ring[4 + 4 * lane + side].wait_recv()
                where = slot(da, -db)
                n = 6 + 4 * lane + side
                ring[n] = ship(n, view(where, side), where, side, on_seq(0, db))

        for side, da in ((0, 1), (1, -1)):
            ring[side].wait_recv()
            where = slot(-da, 0)
            ring[2 + side] = ship(2 + side, view(where, side), where, side, on_seq(da, 0))
            second(1 + side)
            yield
        ring[2].wait_recv()
        ring[3].wait_recv()
        second(3)
        yield
        for lane in range(4):
            onward(lane)
            yield
        for lane in range(4):
            ring[6 + 4 * lane].wait_recv()
            ring[7 + 4 * lane].wait_recv()
        yield

    def basis_view(cols, where, part):
        if part is None:
            return basis.at[pl.ds(pl.multiple_of(160 * where, 32), 160), cols]
        return basis.at[pl.ds(pl.multiple_of(160 * where + 80 * part, 16), 80), cols]

    def own_basis(cols):
        first = parity * HALF + h * QUARTER + cols.start
        return act_basis.at[:, pl.ds(pl.multiple_of(first, 128), cols.size)]

    partner = {"seq": s, "eig": 2 * wrap(y + 2 * lower - 1) + h}

    def share_rows():
        near = rows.at[at_rows(1 + lower)]
        far = rows.at[at_rows(3 * lower)]
        first = remote(
            cand_act.at[0], rows.at[at_rows(3 * (1 - lower))], cs.at[0], cr.at[0], partner
        )
        across = [remote(cand_act.at[0], near, cs.at[1], cr.at[1], sibling)]
        yield
        first.wait_recv()
        across.append(remote(far, far, cs.at[2], cr.at[2], sibling))
        yield
        local[3].wait()
        for copy in across:
            copy.wait_recv()
        yield

    def share_grads():
        grads_in = []
        for offsets in ((2, 6), (3, 5, 4, 1, 7)):
            for d in offsets:
                to = lax.rem(e + d, 8)
                cols = pl.ds(pl.multiple_of(to * GB, 128), GB)
                copy = remote(
                    cand_grad.at[0, :, cols], grads.at[place], gs.at[d], gr.at[d], on_eig(d)
                )
                grads_in.append(copy)
            yield
        local[4].wait()
        for copy in grads_in:
            copy.wait_recv()
        yield

    def rotate_grads():
        next(run["G"])

        def turn(i, carry):
            cols = pl.ds(pl.multiple_of(i * 256, 256), 256)
            turned = mm(grads[...].reshape(LEN, GB), gbasis[:, cols]).astype(BF)
            rot_t[cols, :] = turned.T
            return carry

        for first, last in ((0, 2), (2, 4), (4, 5)):
            lax.fori_loop(first, last, turn, 0)
            yield

    def own_grads():
        local[1].wait()
        local[2].wait()

        def turn(i, carry):
            cols = pl.ds(pl.multiple_of(i * 256, 256), 256)
            turned = mm(raw_grad[...].reshape(128, GB), gbasis[:, cols]).astype(BF)
            all_grad[pl.ds(4 * s, 4), :, cols] = turned.reshape(4, LQ, 256)
            return carry

        lax.fori_loop(0, 5, turn, 0)
        yield

    def grad_view(cols, where, part):
        if part is None:
            return all_grad.at[pl.ds(4 * where, 4), :, cols]
        return all_grad.at[pl.ds(4 * where + 2 * part, 2), :, cols]

    def invert():
        local[5].wait()

        def body(i, carry):
            at = pl.ds(pl.multiple_of(i * 64, 64), 64)
            recip[at, :] = 1.0 / recip[at, :]
            return carry

        for first in range(0, 20, 5):
            lax.fori_loop(first, first + 5, body, 0)
            yield

    mine = pl.ds(pl.multiple_of(h * QUARTER, 128), QUARTER)

    def rotate_rows():
        local[0].wait()
        for copy in local[6:]:
            copy.wait()
        next(run["r"])

        def add(i, carry):
            at = pl.ds(pl.multiple_of(i * 512, 512), 512)
            total[...] += mm(rows[:, at], basis[at, :])
            return carry

        total[...] = jnp.zeros_like(total)
        lax.fori_loop(0, 5, add, 0)
        length = lens[0]
        r = lax.broadcasted_iota(jnp.int32, (128, 1), 0)
        for n, (chip, core) in enumerate(((-1, other), (0, other), (0, parity), (1, parity))):
            token = 256 * wrap(y + chip) + 128 * core + r
            turned = total[128 * n : 128 * n + 128].astype(BF)
            at = pl.ds(pl.multiple_of(256 * wrap(y - 1 + n // 2) + 128 * (n % 2), 128), 128)
            act[parity, at, mine] = jnp.where(token < length, turned, jnp.zeros((), BF))
        slim[pl.ds(4 * s, 4)] = total[512:640].astype(BF).reshape(4, LQ, QUARTER)
        yield

    def act_view(half, block):
        return act.at[half, pl.ds(pl.multiple_of(256 * block, 256), 256), mine]

    def gather_act():
        def ship(n, half, block, device):
            view = act_view(half, block)
            return remote(view, view, as_.at[n], ar.at[n], device)

        ring = {}
        for side, d in ((0, 1), (1, -1)):
            ring[side] = ship(side, parity, wrap(y - 1 + side), on_y(d))
        for side, d in ((0, 1), (1, -1)):
            ring[2 + side] = ship(2 + side, parity, wrap(y - side), on_y(d))
        across = [ship(6 + side, parity, wrap(y - 1 + side), sibling) for side in (0, 1)]
        yield
        for side, d in ((0, 1), (1, -1)):
            ring[side].wait_recv()
            block = wrap(y - d - 1 + side)
            ring[4 + side] = ship(4 + side, other, block, on_y(d))
            across.append(ship(8 + side, other, block, sibling))
        yield
        for side, d in ((0, 1), (1, -1)):
            ring[2 + side].wait_recv()
            across.append(ship(10 + side, other, wrap(y - d - side), sibling))
        yield
        for copy in across[:2]:
            copy.wait_recv()
        yield
        for copy in across[2:6]:
            copy.wait_recv()
        yield
        for side in (0, 1):
            ring[4 + side].wait_recv()
            across.append(ship(12 + side, parity, wrap(y + 1 + side), sibling))
        yield
        for copy in across[6:]:
            copy.wait_recv()
        yield

    def slim_view(cols, where, part):
        if part is None:
            return slim.at[pl.ds(4 * where, 4), :, cols]
        return slim.at[pl.ds(4 * where + 2 * part, 2), :, cols]

    def choose():
        def ship(n, half, piece, device):
            view = chosen.at[half, :, mine]
            if piece is not None:
                view = chosen.at[half, pl.ds(256 * piece, 256), mine]
            return remote(view, view, ts.at[n], tr.at[n], device)

        for k in range(KQ):
            chosen[parity, LQ * k : LQ * k + LQ, mine] = slim[lists[s, k]]
        near = [ship(0, parity, 0, on_y(1)), ship(1, parity, 1, on_y(-1))]
        across = [ship(2, parity, None, sibling)]
        yield
        for side in (0, 1):
            near[side].wait_recv()
            across.append(ship(3 + side, other, side, sibling))
        yield
        for copy in across[1:]:
            copy.wait_recv()
        yield
        across[0].wait_recv()
        yield

    def cross_other():
        def body(i, carry):
            cols = pl.ds(pl.multiple_of(i * 256, 256), 256)
            wide = pl.ds(pl.multiple_of(other * HALF + i * 256, 256), 256)
            block = mm(rot_t[...], act[other, :, cols])
            scaled[other, :, cols] = (block * recip[:, wide]).astype(BF)
            return carry

        for first, last in ((0, 2), (2, 5)):
            lax.fori_loop(first, last, body, 0)
            yield

    def cross_own():
        def two(block, cols):
            at = [pl.ds(pl.multiple_of(256 * wrap(block + n), 256), 256) for n in (0, 1)]
            return mm(rot_t[:, at[0]], act[parity, at[0], cols]) + mm(
                rot_t[:, at[1]], act[parity, at[1], cols]
            )

        def begin(i, carry):
            cols = pl.ds(pl.multiple_of(i * 256, 256), 256)
            begun[:, cols] = two(y - 1, cols)
            return carry

        def finish(i, carry):
            cols = pl.ds(pl.multiple_of(i * 256, 256), 256)
            wide = pl.ds(pl.multiple_of(parity * HALF + i * 256, 256), 256)
            block = begun[:, cols] + two(y + 1, cols)
            scaled[parity, :, cols] = (block * recip[:, wide]).astype(BF)
            return carry

        lax.fori_loop(0, 5, begin, 0)
        yield
        lax.fori_loop(0, 5, finish, 0)
        yield

    def project(half, add):
        next(run["k"])
        block = mm(chosen[half], scaled[half], ((1,), (1,)))
        proj[...] = proj[...] + block if add else block
        yield

    run = {
        "b": torus(basis_view, own_basis, bs, br),
        "r": share_rows(),
        "G": share_grads(),
        "w": own_grads(),
        "g": torus(grad_view, lambda cols: grad_view(cols, s, None), hs, hr, GB),
        "s": torus(slim_view, lambda cols: slim_view(cols, s, None), qs, qr),
        "i": invert(),
        "M": rotate_rows(),
        "a": gather_act(),
        "t": rotate_grads(),
        "k": choose(),
        "x": cross_other(),
        "X": cross_own(),
        "p": project(parity, True),
        "q": project(other, False),
    }
    order = "".join(ORDER)
    for n, letter in enumerate(order):
        if n == 2:
            for copy in local:
                copy.start()
        next(run[letter])
    for stages in run.values():
        assert next(stages, 0) == 0

    def score(k, carry):
        grad = all_grad[lists[s, k]].astype(F32)
        at = pl.ds(pl.multiple_of(LQ * k, LQ), LQ)
        folded = proj[at, :128] * grad[:, :128]
        for n in range(1, GB // 128):
            cols = slice(128 * n, 128 * n + 128)
            folded += proj[at, cols] * grad[:, cols]
        part[e, pl.ds(k, 1), :] = jnp.sum(folded, axis=0, keepdims=True)
        return carry

    lax.fori_loop(0, KQ, score, 0)

    parts_in = [
        remote(part.at[e], part.at[e], ps.at[d], pr.at[d], on_eig(d))
        for d in range(1, 8)
    ]
    for copy in parts_in:
        copy.wait_recv()
    full = part[0]
    for block in range(1, 8):
        full += part[block]
    full = jnp.concatenate([full, jnp.zeros((128 - KQ, 128), F32)], axis=0)
    out[...] = (jnp.sum(full.T, axis=0, keepdims=True) * FACTOR)[:, :KQ]

    for copy in sent:
        copy.wait_send()


def shards(
    cand_act, cand_grad, query_act, query_grad, act_basis, grad_basis, eigvals, query_lists,
    valid_len,
):
    anywhere = pl.BlockSpec(memory_space=pl.ANY)
    scalars = pl.BlockSpec(memory_space=pltpu.SMEM)
    dma = pltpu.SemaphoreType.DMA
    return pl.pallas_call(
        kernel,
        out_shape=jax.ShapeDtypeStruct((1, KQ), F32),
        in_specs=[scalars, scalars] + [anywhere] * 7,
        out_specs=pl.BlockSpec(memory_space=pltpu.VMEM),
        scratch_shapes=[
            pltpu.VMEM((DW, QUARTER), BF),
            pltpu.VMEM((640, DW), BF),
            pltpu.VMEM((640, QUARTER), F32),
            pltpu.VMEM((2, LEN, HALF), BF),
            pltpu.VMEM((8, 128, GB), BF),
            pltpu.VMEM((GB, LEN), BF),
            pltpu.VMEM((GB, GB), BF),
            pltpu.VMEM((GB, DW), F32),
            pltpu.VMEM((2, GB, HALF), BF),
            pltpu.VMEM((64, LQ, GB), BF),
            pltpu.VMEM((64, LQ, QUARTER), BF),
            pltpu.VMEM((2, KQ * LQ, HALF), BF),
            pltpu.VMEM((KQ * LQ, GB), F32),
            pltpu.VMEM((GB, HALF), F32),
            pltpu.VMEM((4, LQ, GB), BF),
            pltpu.VMEM((8, KQ, 128), F32),
            dma((10,)),
            dma((20,)), dma((20,)),
            dma((8,)), dma((8,)),
            dma((3,)), dma((3,)),
            dma((14,)), dma((14,)),
            dma((20,)), dma((20,)),
            dma((20,)), dma((20,)),
            dma((5,)), dma((5,)),
            dma((8,)), dma((8,)),
        ],
        compiler_params=pltpu.CompilerParams(
            collective_id=0, has_side_effects=True, vmem_limit_bytes=63 * 2**20
        ),
        name="influence",
    )(
        query_lists, valid_len, cand_act, cand_grad, query_act, query_grad, act_basis,
        grad_basis, eigvals,
    )


def solution(mesh):
    placed = (
        P("seq", "eig", None),
        P("seq", "eig", None),
        P("seq", None, None),
        P("seq", None, "eig"),
        P("seq", None),
        P("eig", None, None),
        P("eig", None),
        P(),
        P("seq"),
    )
    return jax.shard_map(
        shards, mesh=mesh, in_specs=placed, out_specs=P("seq", None), check_vma=False
    )
```

time: 105 us -> 90.1 us (0.86)
  Pallas kernels: 103 us -> 88.1 us
    pallas_call x1, Pallas kernels: 103 us -> 88.1 us  [shards(): pl.pallas_call(kernel, out_shape=jax.ShapeDtypeStruct((1, KQ), F32), in_s...]
where the time goes in v2:
time: 90.1 us; the launch traced here: 90 us
  Pallas kernels  88.1 us (98%)
  local copies, waits for them, and re-layouts  1.19 us (1%)
    pallas_call x1, Pallas kernels, shards(): pl.pallas_call(kernel, out_shape=jax.ShapeDtypeStruct((1, KQ), F32), in_s...  88.1 us

profile of v2, /device:TPU:1, one launch (start us, length us, event | category | flops | bytes accessed | tf_op | source)
XLA Modules:
  0.0 90.0 jit_solution(14196902855925442349)
XLA Ops:
  0.7 88.1 %influence.1 = f32[1,16]{1,0:T(1,128)} custom-call(s32[16,16]{1,0:T(8,128)} %lists.1, s32[1]{0:T(128)S(6)} %copy.11.lens, bf16[1,128,2560]{2,1,0:T(8,128)(2,1)} %cand_act.1, bf16[1,128,10240]{2,1,0:T(8,128)(2,1)} %cand_grad.1, bf16[4,32,2560]{2,1,0:T(8,128)(2,1)} %query_act.1, bf16[4,32,1280]{2,1,0:T(8,128)(2,1)} %query_grad.1, bf16[160,2560]{1,0:T(8,128)(2,1)} %act_basis.1, ...), custom_call_target="tpu_custom_call" | custom-call | tf_op jit(solution)/shard_map/influence/pallas_call | solution.py:435
  88.8 1.2 %copy.12 = f32[1,16]{1,0:T(1,128)} copy(f32[1,16]{1,0:T(1,128)} %influence.1) | data formatting | bytes 128

commit v3 on v2

--- a/solution.py
+++ b/solution.py
@@ -22,8 +22,8 @@
 FACTOR = 1.0 / math.sqrt(FW * DW * LEN * LQ)
 ORDER = (
     "brGwbbbbirGbbbib",
-    "gMasigissssssagsgskgtg",
-    "tatgaXgaxxkaqaXpg",
+    "gMsigissasssatagtssgskggta",
+    "XgaxaxgakXkpkpg",
 )
 LANES = (0, -1, 1, 2)
 
@@ -278,6 +278,9 @@
             ring[2 + side] = ship(2 + side, parity, wrap(y - side), on_y(d))
         across = [ship(6 + side, parity, wrap(y - 1 + side), sibling) for side in (0, 1)]
         yield
+        for copy in across[:2]:
+            copy.wait_recv()
+        yield
         for side, d in ((0, 1), (1, -1)):
             ring[side].wait_recv()
             block = wrap(y - d - 1 + side)
@@ -287,9 +290,6 @@
         for side, d in ((0, 1), (1, -1)):
             ring[2 + side].wait_recv()
             across.append(ship(10 + side, other, wrap(y - d - side), sibling))
-        yield
-        for copy in across[:2]:
-            copy.wait_recv()
         yield
         for copy in across[2:6]:
             copy.wait_recv()
@@ -319,14 +319,14 @@
         near = [ship(0, parity, 0, on_y(1)), ship(1, parity, 1, on_y(-1))]
         across = [ship(2, parity, None, sibling)]
         yield
+        across[0].wait_recv()
+        yield
         for side in (0, 1):
             near[side].wait_recv()
             across.append(ship(3 + side, other, side, sibling))
         yield
         for copy in across[1:]:
             copy.wait_recv()
-        yield
-        across[0].wait_recv()
         yield
 
     def cross_other():
@@ -365,10 +365,10 @@
         lax.fori_loop(0, 5, finish, 0)
         yield
 
-    def project(half, add):
-        next(run["k"])
-        block = mm(chosen[half], scaled[half], ((1,), (1,)))
-        proj[...] = proj[...] + block if add else block
+    def project():
+        proj[...] = mm(chosen[parity], scaled[parity], ((1,), (1,)))
+        yield
+        proj[...] += mm(chosen[other], scaled[other], ((1,), (1,)))
         yield
 
     run = {
@@ -385,8 +385,7 @@
         "k": choose(),
         "x": cross_other(),
         "X": cross_own(),
-        "p": project(parity, True),
-        "q": project(other, False),
+        "p": project(),
     }
     order = "".join(ORDER)
     for n, letter in enumerate(order):

time: 90.1 us -> 86.8 us (0.963)
  Pallas kernels: 88.1 us -> 84.8 us
    pallas_call x1, Pallas kernels: 88.1 us -> 84.8 us  [shards(): pl.pallas_call(kernel, out_shape=jax.ShapeDtypeStruct((1, KQ), F32), in_s...]
where the time goes in v3:
time: 86.8 us; the launch traced here: 86.6 us
  Pallas kernels  84.8 us (98%)
  local copies, waits for them, and re-layouts  1.19 us (1%)
    pallas_call x1, Pallas kernels, shards(): pl.pallas_call(kernel, out_shape=jax.ShapeDtypeStruct((1, KQ), F32), in_s...  84.8 us

profile of v3, /device:TPU:1, one launch (start us, length us, event | category | flops | bytes accessed | tf_op | source)
XLA Modules:
  0.0 86.6 jit_solution(16467041009436776498)
XLA Ops:
  0.7 84.8 %influence.1 = f32[1,16]{1,0:T(1,128)} custom-call(s32[16,16]{1,0:T(8,128)} %lists.1, s32[1]{0:T(128)S(6)} %copy.11.lens, bf16[1,128,2560]{2,1,0:T(8,128)(2,1)} %cand_act.1, bf16[1,128,10240]{2,1,0:T(8,128)(2,1)} %cand_grad.1, bf16[4,32,2560]{2,1,0:T(8,128)(2,1)} %query_act.1, bf16[4,32,1280]{2,1,0:T(8,128)(2,1)} %query_grad.1, bf16[160,2560]{1,0:T(8,128)(2,1)} %act_basis.1, ...), custom_call_target="tpu_custom_call" | custom-call | tf_op jit(solution)/shard_map/influence/pallas_call | solution.py:434
  85.4 1.2 %copy.12 = f32[1,16]{1,0:T(1,128)} copy(f32[1,16]{1,0:T(1,128)} %influence.1) | data formatting | bytes 128

commit v4 on v3

--- a/solution.py
+++ b/solution.py
@@ -412,6 +412,8 @@
         remote(part.at[e], part.at[e], ps.at[d], pr.at[d], on_eig(d))
         for d in range(1, 8)
     ]
+    for copy in sent:
+        copy.wait_send()
     for copy in parts_in:
         copy.wait_recv()
     full = part[0]
@@ -419,9 +421,6 @@
         full += part[block]
     full = jnp.concatenate([full, jnp.zeros((128 - KQ, 128), F32)], axis=0)
     out[...] = (jnp.sum(full.T, axis=0, keepdims=True) * FACTOR)[:, :KQ]
-
-    for copy in sent:
-        copy.wait_send()
 
 
 def shards(

time: 86.8 us -> 86.6 us (level)
  no operation moved by 1% of the time
where the time goes in v4:
time: 86.6 us; the launch traced here: 86.5 us
  Pallas kernels  84.6 us (98%)
  local copies, waits for them, and re-layouts  1.19 us (1%)
    pallas_call x1, Pallas kernels, shards(): pl.pallas_call(kernel, out_shape=jax.ShapeDtypeStruct((1, KQ), F32), in_s...  84.6 us

profile of v4, /device:TPU:1, one launch (start us, length us, event | category | flops | bytes accessed | tf_op | source)
XLA Modules:
  0.0 86.5 jit_solution(15796329154348172538)
XLA Ops:
  0.7 84.6 %influence.1 = f32[1,16]{1,0:T(1,128)} custom-call(s32[16,16]{1,0:T(8,128)} %lists.1, s32[1]{0:T(128)S(6)} %copy.11.lens, bf16[1,128,2560]{2,1,0:T(8,128)(2,1)} %cand_act.1, bf16[1,128,10240]{2,1,0:T(8,128)(2,1)} %cand_grad.1, bf16[4,32,2560]{2,1,0:T(8,128)(2,1)} %query_act.1, bf16[4,32,1280]{2,1,0:T(8,128)(2,1)} %query_grad.1, bf16[160,2560]{1,0:T(8,128)(2,1)} %act_basis.1, ...), custom_call_target="tpu_custom_call" | custom-call | tf_op jit(solution)/shard_map/influence/pallas_call | solution.py:433
  85.3 1.2 %copy.12 = f32[1,16]{1,0:T(1,128)} copy(f32[1,16]{1,0:T(1,128)} %influence.1) | data formatting | bytes 128
